TPU v7x, 512 devices: a whole 4x8x8 slice. The times are simulated.
512 devices in a mesh: frames: 128 (over z, y, x_lo), heads: 4 (over x_hi, core).
Axes of the slice: x: 4 (x_hi: 2, x_lo: 2; x = x_hi * 2 + x_lo), y: 8, z: 8, core: 2. Of those that a mesh axis runs over, the one named last changes fastest.
Arguments:
- queries: bfloat16 [12288, 2560], P('frames', 'heads'), may hold values from -40 to 40
- keys_values: bfloat16 [2, 12288, 2560], P(None, 'frames', 'heads'), may hold values from -40 to 40
- out_weight: bfloat16 [2560, 5120], P('heads', 'frames'), may hold values from -0.5 to 0.5
Outputs:
- projected: bfloat16 [12288, 5120], P('frames', 'heads')
All inputs are finite; a program needn't handle non-finite values.
Results may differ from a plain program's by a relative error of at most 0.015.
Values may be sent and summed in bfloat16 or wider, within the bound.
A program may use at most 64 MiB of HBM per device.

v0:
```python
import jax
import jax.numpy as jnp
from jax import lax
from jax.sharding import PartitionSpec as P

HD = 128
TPF = 32
FR_DEV = 3


reach_cap = 32


def from_behind(x, axis, by):
    devices = lax.axis_size(axis)
    return lax.ppermute(x, axis, [(i, (i + by) % devices) for i in range(devices)])


def on_device(queries, keys_values, out_weight):
    total_frames = lax.axis_size("frames") * FR_DEV
    reach = min(reach_cap, (total_frames - 1) // 2)
    steps = (reach + FR_DEV - 1) // FR_DEV
    width = keys_values.shape[2]
    span = FR_DEV + 2 * reach
    stacked = keys_values.reshape(2, FR_DEV, TPF, width)
    pieces = []
    for offset in range(-steps, steps + 1):
        if offset == 0:
            pieces.append(stacked)
        else:
            pieces.append(from_behind(stacked, "frames", -offset))
    window = jnp.concatenate(pieces, axis=1)
    lower_frame = steps * FR_DEV - reach
    extended = window[:, lower_frame : lower_frame + span]
    keys_ext = extended[0].reshape(span * TPF, width)
    values_ext = extended[1].reshape(span * TPF, width)
    row_frame = jnp.arange(FR_DEV * TPF, dtype=jnp.int32) // TPF
    col_frame = jnp.arange(span * TPF, dtype=jnp.int32) // TPF
    allowed = (col_frame[None, :] >= row_frame[:, None]) & (
        col_frame[None, :] <= row_frame[:, None] + 2 * reach
    )
    results = []
    for head in range(width // HD):
        lower = head * HD
        query_cols = queries[:, lower : lower + HD]
        key_cols = keys_ext[:, lower : lower + HD]
        scores = lax.dot_general(
            query_cols, key_cols, (((1,), (1,)), ((), ())), preferred_element_type=jnp.float32
        )
        scores = scores * HD ** (-0.5)
        top = jnp.max(jnp.where(allowed, scores, -1e30), axis=1, keepdims=True)
        weights = jnp.where(allowed, jnp.exp(scores - top), 0.0)
        probs = (weights / jnp.sum(weights, axis=1, keepdims=True)).astype(jnp.bfloat16)
        results.append(
            jnp.dot(
                probs, values_ext[:, lower : lower + HD], preferred_element_type=jnp.float32
            ).astype(jnp.bfloat16)
        )
    attended = jnp.concatenate(results, axis=1)
    partial_rows = jnp.dot(
        attended,
        lax.all_gather(out_weight, "frames", axis=1, tiled=True),
        preferred_element_type=jnp.float32,
    )
    return lax.psum_scatter(
        partial_rows.astype(jnp.bfloat16), "heads", scatter_dimension=1, tiled=True
    )


def solution(mesh):
    in_specs = (P("frames", "heads"), P(None, "frames", "heads"), P("heads", "frames"))
    out_specs = P("frames", "heads")
    return jax.shard_map(
        on_device, mesh=mesh, in_specs=in_specs, out_specs=out_specs, check_vma=False
    )
```

profile of v0, /device:TPU:1, one launch (start us, length us, event | category | flops | bytes accessed | tf_op | source)
XLA Modules:
  0.0 740.1 jit_solution(7605853426506819960)
XLA Ops:
  6.5 0.7 all-gather.2.cloned.1.call-update
  7.3 0.0 reduce-scatter.2.cloned.1.call-start
  7.3 8.4 %collective-permute-start = (bf16[2,3,32,640]{3,2,1,0:T(8,128)(2,1)}, bf16[2,3,32,640]{3,2,1,0:T(8,128)(2,1)S(1)}, u32[]{:S(2)}, u32[]{:S(2)}) collective-permute-start(bf16[2,3,32,640]{3,2,1,0:T(8,128)(2,1)} %bitcast.25), channel_id=1, source_target_pairs={{0,44},{4,48},{8,52},{12,56},{16,60},{20,64},{24,68},{28,72},{32,7... | collective-permute-start | bytes 737288 | tf_op jit(solution)/shard_map/ppermute | solution.py:16
  15.7 4.6 collective-permute-start.1
  20.3 4.8 collective-permute-start.2
  25.2 6.2 collective-permute-start.3
  31.4 4.4 collective-permute-start.4
  35.8 0.0 collective-permute-done
  35.8 4.3 collective-permute-start.5
  40.2 8.4 %collective-permute-done.1 = bf16[2,3,32,640]{3,2,1,0:T(8,128)(2,1)S(1)} collective-permute-done((bf16[2,3,32,640]{3,2,1,0:T(8,128)(2,1)}, bf16[2,3,32,640]{3,2,1,0:T(8,128)(2,1)S(1)}, u32[]{:S(2)}, u32[]{:S(2)}) %collective-permute-start.1) | collective-permute-done | bytes 245792 | tf_op jit(solution)/shard_map/ppermute | solution.py:16
  48.6 6.4 collective-permute-start.6
  55.0 6.1 collective-permute-done.2
  61.1 19.7 %collective-permute-start.7 = (bf16[2,3,32,640]{3,2,1,0:T(8,128)(2,1)}, bf16[2,3,32,640]{3,2,1,0:T(8,128)(2,1)S(1)}, u32[]{:S(2)}, u32[]{:S(2)}) collective-permute-start(bf16[2,3,32,640]{3,2,1,0:T(8,128)(2,1)} %bitcast.32), channel_id=1, source_target_pairs={{0,16},{4,20},{8,24},{12,28},{16,32},{20,36},{24,40},{28,44},{32,4... | collective-permute-start | bytes 737288 | tf_op jit(solution)/shard_map/ppermute | solution.py:16
  80.8 0.0 collective-permute-done.3
  80.8 6.9 collective-permute-start.8
  87.8 0.0 collective-permute-done.4
  87.8 6.6 collective-permute-start.9
  94.4 0.0 collective-permute-done.5
  94.4 1.9 collective-permute-start.10
  96.4 0.0 collective-permute-done.6
  96.4 7.6 %collective-permute-start.11 = (bf16[2,3,32,640]{3,2,1,0:T(8,128)(2,1)}, bf16[2,3,32,640]{3,2,1,0:T(8,128)(2,1)S(1)}, u32[]{:S(2)}, u32[]{:S(2)}) collective-permute-start(bf16[2,3,32,640]{3,2,1,0:T(8,128)(2,1)} %bitcast.36), channel_id=1, source_target_pairs={{0,508},{4,0},{8,4},{12,8},{16,12},{20,16},{24,20},{28,24},{32,28}... | collective-permute-start | bytes 737288 | tf_op jit(solution)/shard_map/ppermute | solution.py:16
  104.0 2.6 collective-permute-done.7
  106.6 7.4 %collective-permute-start.12 = (bf16[2,3,32,640]{3,2,1,0:T(8,128)(2,1)}, bf16[2,3,32,640]{3,2,1,0:T(8,128)(2,1)S(1)}, u32[]{:S(2)}, u32[]{:S(2)}) collective-permute-start(bf16[2,3,32,640]{3,2,1,0:T(8,128)(2,1)} %bitcast.37), channel_id=1, source_target_pairs={{0,504},{4,508},{8,0},{12,4},{16,8},{20,12},{24,16},{28,20},{32,24... | collective-permute-start | bytes 737288 | tf_op jit(solution)/shard_map/ppermute | solution.py:16
  114.1 2.5 collective-permute-done.8
  116.6 3.8 collective-permute-start.13
  120.4 0.0 collective-permute-done.9
  120.4 5.2 collective-permute-start.14
  125.7 6.7 collective-permute-done.10
  132.4 1.9 collective-permute-start.15
  134.3 1.0 constant_dynamic-update-slice_fusion.11
  135.3 0.0 collective-permute-done.11
  135.3 7.5 %collective-permute-start.16 = (bf16[2,3,32,640]{3,2,1,0:T(8,128)(2,1)S(1)}, bf16[2,3,32,640]{3,2,1,0:T(8,128)(2,1)S(1)}, u32[]{:S(2)}, u32[]{:S(2)}) collective-permute-start(bf16[2,3,32,640]{3,2,1,0:T(8,128)(2,1)S(1)} %bitcast.42), channel_id=1, source_target_pairs={{0,488},{4,492},{8,496},{12,500},{16,504},{20,508},{24,0},{28,4},{... | collective-permute-start | bytes 737288 | tf_op jit(solution)/shard_map/ppermute | solution.py:16
  142.9 0.0 collective-permute-done.12
  142.9 7.3 collective-permute-start.17
  150.3 0.0 collective-permute-done.13
  150.3 1.9 collective-permute-start.18
  152.2 0.0 collective-permute-done.14
  152.3 2.9 collective-permute-start.19
  155.2 0.0 collective-permute-done.15
  155.2 8.1 %collective-permute-start.20 = (bf16[2,3,32,640]{3,2,1,0:T(8,128)(2,1)S(1)}, bf16[2,3,32,640]{3,2,1,0:T(8,128)(2,1)S(1)}, u32[]{:S(2)}, u32[]{:S(2)}) collective-permute-start(bf16[2,3,32,640]{3,2,1,0:T(8,128)(2,1)S(1)} %bitcast.46), channel_id=1, source_target_pairs={{0,472},{4,476},{8,480},{12,484},{16,488},{20,492},{24,496},{28,50... | collective-permute-start | bytes 737288 | tf_op jit(solution)/shard_map/ppermute | solution.py:16
  163.3 9.2 %collective-permute-done.16 = bf16[2,3,32,640]{3,2,1,0:T(8,128)(2,1)S(1)} collective-permute-done((bf16[2,3,32,640]{3,2,1,0:T(8,128)(2,1)S(1)}, bf16[2,3,32,640]{3,2,1,0:T(8,128)(2,1)S(1)}, u32[]{:S(2)}, u32[]{:S(2)}) %collective-permute-start.16) | collective-permute-done | bytes 245792 | tf_op jit(solution)/shard_map/ppermute | solution.py:16
  172.5 1.9 collective-permute-start.21
  174.5 6.0 collective-permute-done.17
  180.5 0.0 collective-permute-done.18
  180.6 32.5 %collective-permute-done.20 = bf16[2,3,32,640]{3,2,1,0:T(8,128)(2,1)S(1)} collective-permute-done((bf16[2,3,32,640]{3,2,1,0:T(8,128)(2,1)S(1)}, bf16[2,3,32,640]{3,2,1,0:T(8,128)(2,1)S(1)}, u32[]{:S(2)}, u32[]{:S(2)}) %collective-permute-start.20) | collective-permute-done | bytes 245792 | tf_op jit(solution)/shard_map/ppermute | solution.py:16
  213.2 0.0 copy-start.1
  213.2 0.0 collective-permute-done.21
  213.3 0.5 fusion.38
  213.8 0.4 copy-done.1
  214.1 0.3 fusion
  214.4 0.3 fusion.2
  214.8 0.3 fusion.3
  215.1 0.5 select_reduce_fusion
  215.6 1.0 fusion.14
  216.6 0.7 fusion.13
  217.3 0.4 fusion.9
  217.7 0.4 fusion.8
  218.2 0.4 fusion.7
  218.6 0.4 fusion.6
  219.1 0.5 fusion.5
  219.5 395.4 %all-gather.2.cloned.1.call-done = bf16[640,5120]{0,1:T(8,128)(2,1)} async-done(((bf16[640,40]{0,1:T(8,128)(2,1)}), bf16[640,5120]{0,1:T(8,128)(2,1)}) %all-gather.2.cloned.1.call-update) | async-done | bytes 6553616 | tf_op jit(solution)/shard_map/all_gather | solution.py:62
  614.9 5.9 convolution_convert_fusion
  620.9 0.0 reduce-scatter.2.cloned.1.call-update
  620.9 112.4 %reduce-scatter.2.cloned.1.call-done = bf16[96,1280]{1,0:T(8,128)(2,1)} async-done(((bf16[96,5120]{1,0:T(8,128)(2,1)}), bf16[96,1280]{1,0:T(8,128)(2,1)}) %reduce-scatter.2.cloned.1.call-update) | async-done | bytes 245776 | tf_op jit(solution)/shard_map/reduce_scatter | solution.py:65
  (28 shorter events, 0.7 us)
Async XLA Ops:
  6.5 128.8 %copy-start = (bf16[2,96,640]{2,1,0:T(8,128)(2,1)S(1)}, bf16[2,96,640]{2,1,0:T(8,128)(2,1)}, u32[]{:S(2)}) copy-start(bf16[2,96,640]{2,1,0:T(8,128)(2,1)} %param.4) | copy-start | bytes 737284
  6.5 608.4 %all-gather.2.cloned.1.call-start = ((), (), s32[]{:S(2)}) async-start(), calls=%async_computation.1 | async-start | bytes 6604800 | tf_op jit(solution)/shard_map/all_gather | solution.py:62
  7.3 726.0 %reduce-scatter.2.cloned.1.call-start = ((), (), s32[]{:S(2)}) async-start(), calls=%async_computation.2 | async-start | bytes 1228800 | tf_op jit(solution)/shard_map/reduce_scatter | solution.py:65
  7.3 28.5 %collective-permute-start = (bf16[2,3,32,640]{3,2,1,0:T(8,128)(2,1)}, bf16[2,3,32,640]{3,2,1,0:T(8,128)(2,1)S(1)}, u32[]{:S(2)}, u32[]{:S(2)}) collective-permute-start(bf16[2,3,32,640]{3,2,1,0:T(8,128)(2,1)} %bitcast.25), channel_id=1, source_target_pairs={{0,44},{4,48},{8,52},{12,56},{16,60},{20,64},{24,68},{28,72},{32,7... | collective-permute-start | bytes 737288 | tf_op jit(solution)/shard_map/ppermute | solution.py:16
  15.7 32.9 %collective-permute-start.1 = (bf16[2,3,32,640]{3,2,1,0:T(8,128)(2,1)}, bf16[2,3,32,640]{3,2,1,0:T(8,128)(2,1)S(1)}, u32[]{:S(2)}, u32[]{:S(2)}) collective-permute-start(bf16[2,3,32,640]{3,2,1,0:T(8,128)(2,1)} %bitcast.26), channel_id=1, source_target_pairs={{0,40},{4,44},{8,48},{12,52},{16,56},{20,60},{24,64},{28,68},{32,7... | collective-permute-start | bytes 737288 | tf_op jit(solution)/shard_map/ppermute | solution.py:16
  20.3 40.8 %collective-permute-start.2 = (bf16[2,3,32,640]{3,2,1,0:T(8,128)(2,1)}, bf16[2,3,32,640]{3,2,1,0:T(8,128)(2,1)S(1)}, u32[]{:S(2)}, u32[]{:S(2)}) collective-permute-start(bf16[2,3,32,640]{3,2,1,0:T(8,128)(2,1)} %bitcast.27), channel_id=1, source_target_pairs={{0,36},{4,40},{8,44},{12,48},{16,52},{20,56},{24,60},{28,64},{32,6... | collective-permute-start | bytes 737288 | tf_op jit(solution)/shard_map/ppermute | solution.py:16
  25.2 55.7 %collective-permute-start.3 = (bf16[2,3,32,640]{3,2,1,0:T(8,128)(2,1)}, bf16[2,3,32,640]{3,2,1,0:T(8,128)(2,1)S(1)}, u32[]{:S(2)}, u32[]{:S(2)}) collective-permute-start(bf16[2,3,32,640]{3,2,1,0:T(8,128)(2,1)} %bitcast.28), channel_id=1, source_target_pairs={{0,32},{4,36},{8,40},{12,44},{16,48},{20,52},{24,56},{28,60},{32,6... | collective-permute-start | bytes 737288 | tf_op jit(solution)/shard_map/ppermute | solution.py:16
  31.4 56.4 %collective-permute-start.4 = (bf16[2,3,32,640]{3,2,1,0:T(8,128)(2,1)}, bf16[2,3,32,640]{3,2,1,0:T(8,128)(2,1)S(1)}, u32[]{:S(2)}, u32[]{:S(2)}) collective-permute-start(bf16[2,3,32,640]{3,2,1,0:T(8,128)(2,1)} %bitcast.29), channel_id=1, source_target_pairs={{0,28},{4,32},{8,36},{12,40},{16,44},{20,48},{24,52},{28,56},{32,6... | collective-permute-start | bytes 737288 | tf_op jit(solution)/shard_map/ppermute | solution.py:16
  35.8 58.6 %collective-permute-start.5 = (bf16[2,3,32,640]{3,2,1,0:T(8,128)(2,1)}, bf16[2,3,32,640]{3,2,1,0:T(8,128)(2,1)S(1)}, u32[]{:S(2)}, u32[]{:S(2)}) collective-permute-start(bf16[2,3,32,640]{3,2,1,0:T(8,128)(2,1)} %bitcast.30), channel_id=1, source_target_pairs={{0,24},{4,28},{8,32},{12,36},{16,40},{20,44},{24,48},{28,52},{32,5... | collective-permute-start | bytes 737288 | tf_op jit(solution)/shard_map/ppermute | solution.py:16
  48.6 47.8 %collective-permute-start.6 = (bf16[2,3,32,640]{3,2,1,0:T(8,128)(2,1)}, bf16[2,3,32,640]{3,2,1,0:T(8,128)(2,1)S(1)}, u32[]{:S(2)}, u32[]{:S(2)}) collective-permute-start(bf16[2,3,32,640]{3,2,1,0:T(8,128)(2,1)} %bitcast.31), channel_id=1, source_target_pairs={{0,20},{4,24},{8,28},{12,32},{16,36},{20,40},{24,44},{28,48},{32,5... | collective-permute-start | bytes 737288 | tf_op jit(solution)/shard_map/ppermute | solution.py:16
  61.1 45.5 %collective-permute-start.7 = (bf16[2,3,32,640]{3,2,1,0:T(8,128)(2,1)}, bf16[2,3,32,640]{3,2,1,0:T(8,128)(2,1)S(1)}, u32[]{:S(2)}, u32[]{:S(2)}) collective-permute-start(bf16[2,3,32,640]{3,2,1,0:T(8,128)(2,1)} %bitcast.32), channel_id=1, source_target_pairs={{0,16},{4,20},{8,24},{12,28},{16,32},{20,36},{24,40},{28,44},{32,4... | collective-permute-start | bytes 737288 | tf_op jit(solution)/shard_map/ppermute | solution.py:16
  80.8 35.7 %collective-permute-start.8 = (bf16[2,3,32,640]{3,2,1,0:T(8,128)(2,1)}, bf16[2,3,32,640]{3,2,1,0:T(8,128)(2,1)S(1)}, u32[]{:S(2)}, u32[]{:S(2)}) collective-permute-start(bf16[2,3,32,640]{3,2,1,0:T(8,128)(2,1)} %bitcast.33), channel_id=1, source_target_pairs={{0,12},{4,16},{8,20},{12,24},{16,28},{20,32},{24,36},{28,40},{32,4... | collective-permute-start | bytes 737288 | tf_op jit(solution)/shard_map/ppermute | solution.py:16
  87.8 32.6 %collective-permute-start.9 = (bf16[2,3,32,640]{3,2,1,0:T(8,128)(2,1)}, bf16[2,3,32,640]{3,2,1,0:T(8,128)(2,1)S(1)}, u32[]{:S(2)}, u32[]{:S(2)}) collective-permute-start(bf16[2,3,32,640]{3,2,1,0:T(8,128)(2,1)} %bitcast.34), channel_id=1, source_target_pairs={{0,8},{4,12},{8,16},{12,20},{16,24},{20,28},{24,32},{28,36},{32,40... | collective-permute-start | bytes 737288 | tf_op jit(solution)/shard_map/ppermute | solution.py:16
  94.4 37.9 %collective-permute-start.10 = (bf16[2,3,32,640]{3,2,1,0:T(8,128)(2,1)}, bf16[2,3,32,640]{3,2,1,0:T(8,128)(2,1)S(1)}, u32[]{:S(2)}, u32[]{:S(2)}) collective-permute-start(bf16[2,3,32,640]{3,2,1,0:T(8,128)(2,1)} %bitcast.35), channel_id=1, source_target_pairs={{0,4},{4,8},{8,12},{12,16},{16,20},{20,24},{24,28},{28,32},{32,36}... | collective-permute-start | bytes 737288 | tf_op jit(solution)/shard_map/ppermute | solution.py:16
  96.4 38.9 %collective-permute-start.11 = (bf16[2,3,32,640]{3,2,1,0:T(8,128)(2,1)}, bf16[2,3,32,640]{3,2,1,0:T(8,128)(2,1)S(1)}, u32[]{:S(2)}, u32[]{:S(2)}) collective-permute-start(bf16[2,3,32,640]{3,2,1,0:T(8,128)(2,1)} %bitcast.36), channel_id=1, source_target_pairs={{0,508},{4,0},{8,4},{12,8},{16,12},{20,16},{24,20},{28,24},{32,28}... | collective-permute-start | bytes 737288 | tf_op jit(solution)/shard_map/ppermute | solution.py:16
  106.6 36.3 %collective-permute-start.12 = (bf16[2,3,32,640]{3,2,1,0:T(8,128)(2,1)}, bf16[2,3,32,640]{3,2,1,0:T(8,128)(2,1)S(1)}, u32[]{:S(2)}, u32[]{:S(2)}) collective-permute-start(bf16[2,3,32,640]{3,2,1,0:T(8,128)(2,1)} %bitcast.37), channel_id=1, source_target_pairs={{0,504},{4,508},{8,0},{12,4},{16,8},{20,12},{24,16},{28,20},{32,24... | collective-permute-start | bytes 737288 | tf_op jit(solution)/shard_map/ppermute | solution.py:16
  116.6 33.7 %collective-permute-start.13 = (bf16[2,3,32,640]{3,2,1,0:T(8,128)(2,1)}, bf16[2,3,32,640]{3,2,1,0:T(8,128)(2,1)S(1)}, u32[]{:S(2)}, u32[]{:S(2)}) collective-permute-start(bf16[2,3,32,640]{3,2,1,0:T(8,128)(2,1)} %bitcast.38), channel_id=1, source_target_pairs={{0,500},{4,504},{8,508},{12,0},{16,4},{20,8},{24,12},{28,16},{32,2... | collective-permute-start | bytes 737288 | tf_op jit(solution)/shard_map/ppermute | solution.py:16
  120.4 31.9 %collective-permute-start.14 = (bf16[2,3,32,640]{3,2,1,0:T(8,128)(2,1)}, bf16[2,3,32,640]{3,2,1,0:T(8,128)(2,1)S(1)}, u32[]{:S(2)}, u32[]{:S(2)}) collective-permute-start(bf16[2,3,32,640]{3,2,1,0:T(8,128)(2,1)} %bitcast.39), channel_id=1, source_target_pairs={{0,496},{4,500},{8,504},{12,508},{16,0},{20,4},{24,8},{28,12},{32,... | collective-permute-start | bytes 737288 | tf_op jit(solution)/shard_map/ppermute | solution.py:16
  132.4 22.8 %collective-permute-start.15 = (bf16[2,3,32,640]{3,2,1,0:T(8,128)(2,1)}, bf16[2,3,32,640]{3,2,1,0:T(8,128)(2,1)S(1)}, u32[]{:S(2)}, u32[]{:S(2)}) collective-permute-start(bf16[2,3,32,640]{3,2,1,0:T(8,128)(2,1)} %bitcast.40), channel_id=1, source_target_pairs={{0,492},{4,496},{8,500},{12,504},{16,508},{20,0},{24,4},{28,8},{32... | collective-permute-start | bytes 737288 | tf_op jit(solution)/shard_map/ppermute | solution.py:16
  135.3 37.2 %collective-permute-start.16 = (bf16[2,3,32,640]{3,2,1,0:T(8,128)(2,1)S(1)}, bf16[2,3,32,640]{3,2,1,0:T(8,128)(2,1)S(1)}, u32[]{:S(2)}, u32[]{:S(2)}) collective-permute-start(bf16[2,3,32,640]{3,2,1,0:T(8,128)(2,1)S(1)} %bitcast.42), channel_id=1, source_target_pairs={{0,488},{4,492},{8,496},{12,500},{16,504},{20,508},{24,0},{28,4},{... | collective-permute-start | bytes 737288 | tf_op jit(solution)/shard_map/ppermute | solution.py:16
  142.9 37.6 %collective-permute-start.17 = (bf16[2,3,32,640]{3,2,1,0:T(8,128)(2,1)S(1)}, bf16[2,3,32,640]{3,2,1,0:T(8,128)(2,1)S(1)}, u32[]{:S(2)}, u32[]{:S(2)}) collective-permute-start(bf16[2,3,32,640]{3,2,1,0:T(8,128)(2,1)S(1)} %bitcast.43), channel_id=1, source_target_pairs={{0,484},{4,488},{8,492},{12,496},{16,500},{20,504},{24,508},{28,0}... | collective-permute-start | bytes 737288 | tf_op jit(solution)/shard_map/ppermute | solution.py:16
  150.3 30.3 %collective-permute-start.18 = (bf16[2,3,32,640]{3,2,1,0:T(8,128)(2,1)S(1)}, bf16[2,3,32,640]{3,2,1,0:T(8,128)(2,1)S(1)}, u32[]{:S(2)}, u32[]{:S(2)}) collective-permute-start(bf16[2,3,32,640]{3,2,1,0:T(8,128)(2,1)S(1)} %bitcast.44), channel_id=1, source_target_pairs={{0,480},{4,484},{8,488},{12,492},{16,496},{20,500},{24,504},{28,50... | collective-permute-start | bytes 737288 | tf_op jit(solution)/shard_map/ppermute | solution.py:16
  152.3 28.3 %collective-permute-start.19 = (bf16[2,3,32,640]{3,2,1,0:T(8,128)(2,1)S(1)}, bf16[2,3,32,640]{3,2,1,0:T(8,128)(2,1)S(1)}, u32[]{:S(2)}, u32[]{:S(2)}) collective-permute-start(bf16[2,3,32,640]{3,2,1,0:T(8,128)(2,1)S(1)} %bitcast.45), channel_id=1, source_target_pairs={{0,476},{4,480},{8,484},{12,488},{16,492},{20,496},{24,500},{28,50... | collective-permute-start | bytes 737288 | tf_op jit(solution)/shard_map/ppermute | solution.py:16
  155.2 58.0 %collective-permute-start.20 = (bf16[2,3,32,640]{3,2,1,0:T(8,128)(2,1)S(1)}, bf16[2,3,32,640]{3,2,1,0:T(8,128)(2,1)S(1)}, u32[]{:S(2)}, u32[]{:S(2)}) collective-permute-start(bf16[2,3,32,640]{3,2,1,0:T(8,128)(2,1)S(1)} %bitcast.46), channel_id=1, source_target_pairs={{0,472},{4,476},{8,480},{12,484},{16,488},{20,492},{24,496},{28,50... | collective-permute-start | bytes 737288 | tf_op jit(solution)/shard_map/ppermute | solution.py:16
  172.5 40.7 %collective-permute-start.21 = (bf16[2,3,32,640]{3,2,1,0:T(8,128)(2,1)S(1)}, bf16[2,3,32,640]{3,2,1,0:T(8,128)(2,1)S(1)}, u32[]{:S(2)}, u32[]{:S(2)}) collective-permute-start(bf16[2,3,32,640]{3,2,1,0:T(8,128)(2,1)S(1)} %bitcast.47), channel_id=1, source_target_pairs={{0,468},{4,472},{8,476},{12,480},{16,484},{20,488},{24,492},{28,49... | collective-permute-start | bytes 737288 | tf_op jit(solution)/shard_map/ppermute | solution.py:16
  213.2 0.9 copy-start.1
Sparse Core Ops, SparseCore 0:
  9.4 605.4 all-gather.1
  621.0 112.2 reduce-scatter.1
where the time goes:
time: 741 us; the launch traced here: 740 us
  waiting for transfers between devices  582 us (79%)
  starting transfers between devices  130 us (18%)
  between operations  14 us (2%)
  matrix products  10.6 us (1%)
    all_gather x1, waiting for transfers between devices, on_device(): lax.all_gather(out_weight, 'frames', axis=1, tiled=True)  395 us
    ppermute x22, starting transfers between devices, from_behind(): lax.ppermute(x, axis, [(i, (i + by) % devices) for i in range(devices)])  130 us
    reduce_scatter x1, waiting for transfers between devices, on_device(): lax.psum_scatter(partial_rows.astype(jnp.bfloat16), 'heads', scatter_dime...  112 us
    ppermute x22, waiting for transfers between devices, from_behind(): lax.ppermute(x, axis, [(i, (i + by) % devices) for i in range(devices)])  74 us
  transfers between devices with their start and end apart: 24, of which 10 were waited for; matrix products, arithmetic and copies ran while one was open for 1% of the time, Pallas kernels for 0%

commit v1 on v0

v1 whole, which is shorter than its diff:
```python
import jax
import jax.numpy as jnp
from jax import lax
from jax.experimental import pallas as pl
from jax.experimental.pallas import tpu as pltpu
from jax.sharding import PartitionSpec as P

HD = 128
TPF = 32
NY = 8
NZ = 8
LOCAL_HEADS = 5
ROWS = 96
UNIT = 768
WINDOW = 2816
SUB = 256
KEYS = 2304
COLS = 40
PADDED = 48
KA = 256
KB = 384
NEG = -1e30
LOGE = 1.4426950408889634
MESH = pl.DeviceIdType.MESH


def on_core(q_ref, kv_ref, w_ref, out_ref,
            kv_win, q_win, o_buf, scores, a_buf, wa, wb, part, c_in, summed, x_in, spread,
            p1_s, kv_r, q_r, h_s, h_r, w1_s, w1_r, w2_s, w2_r, o_s, o_r, c_s, c_r, x_s, x_r):
    frames = lax.axis_index("frames")
    heads = lax.axis_index("heads")
    xl = lax.rem(frames, 2)
    y = lax.rem(lax.div(frames, 2), NY)
    z = lax.div(frames, 2 * NY)
    xh = lax.div(heads, 2)
    core = lax.rem(heads, 2)

    def dev(zz, yy, xx, hh, cc):
        return ((zz * NY + yy) * 2 + xx, hh * 2 + cc)

    def remote(src, dst, send, recv, device):
        return pltpu.make_async_remote_copy(
            src_ref=src, dst_ref=dst, send_sem=send, recv_sem=recv,
            device_id=device, device_id_type=MESH)

    mine = (y * 2 + xl) * 2 + core
    partner = dev(z, y, xl, xh, 1 - core)
    barrier = pltpu.get_barrier_semaphore()

    def greet(device):
        pl.semaphore_signal(barrier, inc=1, device_id=device, device_id_type=MESH)

    for k in range(1, 32):
        other = lax.rem(mine + k, 32)
        greet(dev(z, lax.div(other, 4), lax.rem(lax.div(other, 2), 2), xh, lax.rem(other, 2)))
    for k in range(1, NZ):
        greet(dev(lax.rem(z + k, NZ), y, xl, xh, core))
    for k in (1, NZ - 1):
        greet(dev(lax.rem(z + k, NZ), y, xl, xh, 1 - core))
    for k in (0, 1):
        greet(dev(z, y, k, 1 - xh, core))
    pl.semaphore_wait(barrier, 31 + 7 + 2 + 2)

    slot = lax.rem(y, 4) * 2 + xl
    dest_core = lax.div(y, 4)
    selves = []
    for a in range(LOCAL_HEADS):
        place = lax.div((core * LOCAL_HEADS + a) * 8, 5)
        yd, xd = lax.div(place, 2), lax.rem(place, 2)
        to_self = (yd == y) & (xd == xl) & (dest_core == core)
        selves.append(to_self)
        target = dev(z, yd, xd, xh, dest_core)
        kv_src = kv_ref.at[:, :, pl.ds(a * HD, HD)]
        q_src = q_ref.at[:, pl.ds(a * HD, HD)]
        kv_dst = kv_win.at[:, pl.ds(pl.multiple_of(1024 + slot * ROWS, 32), ROWS), :]
        q_dst = q_win.at[pl.ds(pl.multiple_of(slot * ROWS, 32), ROWS), :]

        @pl.when(to_self)
        def _():
            pltpu.make_async_copy(kv_src, kv_dst, kv_r.at[slot]).start()
            pltpu.make_async_copy(q_src, q_dst, q_r.at[slot]).start()

        @pl.when(jnp.logical_not(to_self))
        def _():
            remote(kv_src, kv_dst, p1_s.at[a], kv_r.at[slot], target).start()
            remote(q_src, q_dst, p1_s.at[LOCAL_HEADS + a], q_r.at[slot], target).start()

    wa[z, y] = w_ref[:, :KA]
    wb[z, y] = w_ref[:, KA:]
    for k in range(1, NZ):
        remote(wa.at[z, y], wa.at[z, y], w1_s.at[k - 1], w1_r.at[k - 1],
               dev(lax.rem(z + k, NZ), y, xl, xh, core)).start()
        remote(wb.at[z, y], wb.at[z, y], w1_s.at[6 + k], w1_r.at[6 + k],
               dev(z, lax.rem(y + k, NY), xl, xh, core)).start()

    place = y * 2 + xl
    head = lax.div(place * 5 + 7, 8)
    active = lax.div(head * 8, 5) == place
    unit = z * 2 + core

    def unit_dev(shift):
        other = lax.rem(unit + shift + 16, 16)
        return dev(lax.div(other, 2), y, xl, xh, lax.rem(other, 2))

    halos = (
        (1024, UNIT, 256, 1),
        (1024, UNIT, 1792, -1),
        (1536, 256, 0, 2),
        (1024, 256, 2560, -2),
    )

    def halo(i):
        start, size, to, shift = halos[i]
        return remote(kv_win.at[:, pl.ds(start, size), :], kv_win.at[:, pl.ds(to, size), :],
                      h_s.at[i], h_r.at[i], unit_dev(shift))

    @pl.when(active)
    def _():
        for j in range(8):
            remote(kv_win.at[:, pl.ds(1024 + j * ROWS, ROWS), :],
                   kv_win.at[:, pl.ds(1024 + j * ROWS, ROWS), :],
                   kv_r.at[j], kv_r.at[j], partner).wait_recv()
        for i in range(4):
            halo(i).start()

    sign = 1 - 2 * core

    def ring(i):
        along_y = i < 7
        t = i if along_y else i - 7
        long = t < 4
        t = t if long else t - 4
        way = sign if long else -sign
        if along_y:
            block = lax.rem(y - way * t + 2 * NY, NY)
            target = dev(z, lax.rem(y + way + NY, NY), xl, xh, core)
            ref = wa.at[:, block]
        else:
            block = lax.rem(z - way * t + 2 * NZ, NZ)
            target = dev(lax.rem(z + way + NZ, NZ), y, xl, xh, core)
            ref = wb.at[block]
        return remote(ref, ref, w2_s.at[i], w2_r.at[i], target)

    def ring_arrival(i):
        along_y = i < 7
        t = i if along_y else i - 7
        long = t < 4
        t = t if long else t - 4
        way = sign if long else -sign
        if along_y:
            ref = wa.at[:, lax.rem(y - way * (t + 1) + 2 * NY, NY)]
        else:
            ref = wb.at[lax.rem(z - way * (t + 1) + 2 * NZ, NZ)]
        remote(ref, ref, w2_r.at[i], w2_r.at[i], partner).wait_recv()

    for k in range(1, NZ):
        back = lax.rem(z - k + NZ, NZ)
        remote(wa.at[back, y], wa.at[back, y], w1_r.at[k - 1], w1_r.at[k - 1], partner).wait_recv()
    ring(0).start()
    ring(4).start()
    for k in range(1, NY):
        back = lax.rem(y - k + NY, NY)
        remote(wb.at[z, back], wb.at[z, back], w1_r.at[6 + k], w1_r.at[6 + k], partner).wait_recv()
    ring(7).start()
    ring(11).start()

    def ring_step(t):
        for first, last in ((0, 3), (4, 6), (7, 10), (11, 13)):
            i = first + t
            if i < last:
                ring_arrival(i)
                ring(i + 1).start()
            elif i == last:
                ring_arrival(i)

    def attend(s):
        queries = q_win[pl.ds(s * SUB, SUB), :]
        top = jnp.full((SUB, 256), NEG, jnp.float32)
        rows = lax.broadcasted_iota(jnp.int32, (SUB, 256), 0) // TPF
        cols = lax.broadcasted_iota(jnp.int32, (SUB, 256), 1) // TPF
        for n in range(KEYS // 256):
            keys = kv_win[0, pl.ds(s * SUB + n * 256, 256), :]
            block = lax.dot_general(queries, keys, (((1,), (1,)), ((), ())),
                                    preferred_element_type=jnp.float32)
            if n == 0:
                block = jnp.where(cols >= rows, block, NEG)
            elif n == KEYS // 256 - 1:
                block = jnp.where(cols <= rows, block, NEG)
            scores[:, pl.ds(n * 256, 256)] = block
            top = jnp.maximum(top, block)
        peak = jnp.max(top, axis=1, keepdims=True)
        total = jnp.zeros((SUB, 256), jnp.float32)
        acc = jnp.zeros((SUB, HD), jnp.float32)
        for n in range(KEYS // 256):
            weights = jnp.exp2((scores[:, pl.ds(n * 256, 256)] - peak) * (LOGE * HD ** -0.5))
            total = total + weights
            values = kv_win[1, pl.ds(s * SUB + n * 256, 256), :]
            acc = acc + jnp.dot(weights.astype(jnp.bfloat16), values,
                                preferred_element_type=jnp.float32)
        norm = jnp.sum(total, axis=1, keepdims=True)
        o_buf[pl.ds(s * SUB, SUB), :] = (acc / norm).astype(jnp.bfloat16)

    home_core = lax.div(head, LOCAL_HEADS)
    home_head = lax.rem(head, LOCAL_HEADS)

    def home(r, xx):
        yy = core * 4 + r
        own = (yy == y) & (xx == xl) & (home_core == core)
        src = o_buf.at[pl.ds(r * 192, 192), :]
        dst = a_buf.at[:, pl.ds(pl.multiple_of(home_head * HD, HD), HD)]
        return own, src, dst, dev(z, yy, xx, xh, home_core)

    def send_rows(r):
        for xx in (0, 1):
            own, src, dst, target = home(r, xx)

            @pl.when(own)
            def _():
                pltpu.make_async_copy(src, dst, o_r.at[home_head]).start()

            @pl.when(jnp.logical_not(own))
            def _():
                remote(src, dst, o_s.at[r * 2 + xx], o_r.at[home_head], target).start()

    @pl.when(active)
    def _():
        for j in range(8):
            ref = q_win.at[pl.ds(j * ROWS, ROWS), :]
            remote(ref, ref, q_r.at[j], q_r.at[j], partner).wait_recv()
        for i in range(4):
            halo(i).wait_recv()

    for s in range(3):
        @pl.when(active)
        def _():
            attend(s)
            for r in ((0,), (1,), (2, 3))[s]:
                send_rows(r)
        ring_step(s)

    for k in range(2):
        for yy in range(NY):
            rows = lax.broadcasted_iota(jnp.int32, (PADDED, 640), 0)
            cols = lax.broadcasted_iota(jnp.int32, (PADDED, 640), 1)
            hit = (rows < COLS) & (cols == rows + (2 * yy + k) * COLS)
            spread[pl.ds(k * 384 + yy * PADDED, PADDED), :] = jnp.where(hit, 1.0, 0.0).astype(jnp.bfloat16)

    ring_step(3)

    for a in range(LOCAL_HEADS):
        ref = a_buf.at[:, pl.ds(a * HD, HD)]
        remote(ref, ref, o_r.at[a], o_r.at[a], partner).wait_recv()

    def project(block):
        first = wa[pl.ds(block * 2, 2)].reshape(768, KA)
        second = wb[pl.ds(block * 2, 2)].reshape(768, KB)
        dims = (((1,), (1,)), ((), ()))
        return (lax.dot_general(a_buf[:, :KA], first, dims, preferred_element_type=jnp.float32)
                + lax.dot_general(a_buf[:, KA:], second, dims, preferred_element_type=jnp.float32))

    for k in (0, 1):
        part[k] = project(2 * k + 1 - core).astype(jnp.bfloat16)
        remote(part.at[k], c_in.at[k], c_s.at[k], c_r.at[k], partner).start()

    out_slot = xh * 2 + xl

    def scatter(kh, kl):
        src = summed.at[kh, pl.ds(kl * ROWS, ROWS), :]
        return remote(src, x_in.at[out_slot], x_s.at[kh * 2 + kl], x_r.at[out_slot],
                      dev(z, y, kl, kh, core))

    for k in (0, 1):
        own = project(2 * k + core)
        remote(part.at[k], c_in.at[k], c_s.at[k], c_r.at[k], partner).wait_recv()
        summed[k] = (own + c_in[k].astype(jnp.float32)).astype(jnp.bfloat16)
        for kl in (0, 1):
            here = (k == xh) & (kl == xl)

            @pl.when(here)
            def _():
                x_in[out_slot] = summed[k, pl.ds(kl * ROWS, ROWS), :]

            @pl.when(jnp.logical_not(here))
            def _():
                scatter(k, kl).start()

    for i in range(4):
        @pl.when(i != out_slot)
        def _():
            remote(x_in.at[i], x_in.at[i], x_r.at[i], x_r.at[i], partner).wait_recv()
    for half in (0, 1):
        total = None
        for i in range(4):
            kl = i % 2
            piece = jnp.dot(x_in[i, :, pl.ds(half * 384, 384)], spread[pl.ds(kl * 384, 384), :],
                            preferred_element_type=jnp.float32)
            total = piece if total is None else total + piece
        out_ref[:, pl.ds(half * 640, 640)] = total.astype(jnp.bfloat16)

    for a in range(LOCAL_HEADS):
        @pl.when(jnp.logical_not(selves[a]))
        def _():
            kv_src = kv_ref.at[:, :, pl.ds(a * HD, HD)]
            q_src = q_ref.at[:, pl.ds(a * HD, HD)]
            remote(kv_src, kv_src, p1_s.at[a], p1_s.at[a], partner).wait_send()
            remote(q_src, q_src, p1_s.at[LOCAL_HEADS + a], p1_s.at[LOCAL_HEADS + a], partner).wait_send()
    for i in range(14):
        ref = wa.at[z, y] if i < 7 else wb.at[z, y]
        remote(ref, ref, w1_s.at[i], w1_s.at[i], partner).wait_send()
        ring(i).wait_send()

    @pl.when(active)
    def _():
        for i in range(4):
            halo(i).wait_send()
        for r in range(4):
            for xx in (0, 1):
                own, src, dst, target = home(r, xx)

                @pl.when(jnp.logical_not(own))
                def _():
                    remote(src, dst, o_s.at[r * 2 + xx], o_s.at[r * 2 + xx], target).wait_send()
    for k in (0, 1):
        remote(part.at[k], c_in.at[k], c_s.at[k], c_r.at[k], partner).wait_send()
    for kh in (0, 1):
        for kl in (0, 1):
            @pl.when(jnp.logical_not((kh == xh) & (kl == xl)))
            def _():
                scatter(kh, kl).wait_send()


def on_device(queries, keys_values, out_weight):
    weight = jnp.pad(out_weight.T, ((0, PADDED - COLS), (0, 0)))
    bf16 = jnp.bfloat16
    vmem = pl.BlockSpec(memory_space=pltpu.VMEM)
    dma = pltpu.SemaphoreType.DMA
    return pl.pallas_call(
        on_core,
        out_shape=jax.ShapeDtypeStruct((ROWS, 1280), bf16),
        in_specs=[vmem] * 3,
        out_specs=vmem,
        scratch_shapes=[
            pltpu.VMEM((2, WINDOW, HD), bf16),
            pltpu.VMEM((UNIT, HD), bf16),
            pltpu.VMEM((UNIT, HD), bf16),
            pltpu.VMEM((SUB, KEYS), jnp.float32),
            pltpu.VMEM((192, 640), bf16),
            pltpu.VMEM((NZ, NY, PADDED, KA), bf16),
            pltpu.VMEM((NZ, NY, PADDED, KB), bf16),
            pltpu.VMEM((2, 192, 768), bf16),
            pltpu.VMEM((2, 192, 768), bf16),
            pltpu.VMEM((2, 192, 768), bf16),
            pltpu.VMEM((4, ROWS, 768), bf16),
            pltpu.VMEM((768, 640), bf16),
            dma((10,)), dma((8,)), dma((8,)), dma((4,)), dma((4,)),
            dma((14,)), dma((14,)), dma((14,)), dma((14,)),
            dma((8,)), dma((5,)), dma((2,)), dma((2,)), dma((4,)), dma((4,)),
        ],
        compiler_params=pltpu.CompilerParams(
            collective_id=0, has_side_effects=True, vmem_limit_bytes=48 * 2 ** 20),
        cost_estimate=pl.CostEstimate(flops=2 * 10 ** 9, bytes_accessed=10 ** 6, transcendentals=2 * 10 ** 6),
        name="band_block",
    )(queries, keys_values, weight)


def solution(mesh):
    in_specs = (P("frames", "heads"), P(None, "frames", "heads"), P("heads", "frames"))
    out_specs = P("frames", "heads")
    return jax.shard_map(
        on_device, mesh=mesh, in_specs=in_specs, out_specs=out_specs, check_vma=False
    )
```

time: 741 us -> 81.4 us (0.11)
  waiting for transfers between devices: 582 us -> 0 us
  starting transfers between devices: 130 us -> 0 us
  Pallas kernels: 0 us -> 77.6 us
  between operations: 14 us -> 0.01 us
  matrix products: 10.6 us -> 0 us
    all_gather x1 -> x0, waiting for transfers between devices: 395 us -> none  [on_device(): lax.all_gather(out_weight, 'frames', axis=1, tiled=True)]
    ppermute x22 -> x0, starting transfers between devices: 130 us -> none  [from_behind(): lax.ppermute(x, axis, [(i, (i + by) % devices) for i in range(devices)])]
    reduce_scatter x1 -> x0, waiting for transfers between devices: 112 us -> none  [on_device(): lax.psum_scatter(partial_rows.astype(jnp.bfloat16), 'heads', scatter_dime...]
    pallas_call x0 -> x1, Pallas kernels: none -> 77.6 us  [on_device(): pl.pallas_call(on_core, out_shape=jax.ShapeDtypeStruct((ROWS, 1280), bf16...]
    ppermute x22 -> x0, waiting for transfers between devices: 74 us -> none  [from_behind(): lax.ppermute(x, axis, [(i, (i + by) % devices) for i in range(devices)])]
    dot_general x11 -> x0, matrix products: 10.6 us -> none  [the longest x1 5.94 us: on_device(): jnp.dot(attended, lax.all_gather(out_weight, 'frames', axis=1, tiled=True...]
  transfers between devices with their start and end apart: 24 -> 0, of which waited for: 10 -> 0; matrix products, arithmetic and copies ran while one was open for 1% -> 0% of each run, Pallas kernels for 0% -> 0%
where the time goes in v1:
time: 81.4 us; the launch traced here: 80.9 us
  Pallas kernels  77.6 us (95%)
  local copies, waits for them, and re-layouts  3.35 us (4%)
    pallas_call x1, Pallas kernels, on_device(): pl.pallas_call(on_core, out_shape=jax.ShapeDtypeStruct((ROWS, 1280), bf16...  77.6 us
    unnamed x5, local copies, waits for them, and re-layouts  2.54 us

profile of v1, /device:TPU:1, one launch (start us, length us, event | category | flops | bytes accessed | tf_op | source)
XLA Modules:
  0.0 80.9 jit_solution(2658676033532274836)
XLA Ops:
  0.0 0.8 %pad.4.w_ref = bf16[48,640]{1,0:T(8,128)(2,1)S(1)} pad(bf16[40,640]{1,0:T(8,128)(2,1)} %bitcast.1, bf16[]{:T(256)} %constant.2.clone.1), padding=0_8x0_0 | pad | bytes 112642 | tf_op jit(solution)/shard_map/jit(_pad)/pad | solution.py:333
  0.8 0.0 copy-start
  0.8 0.9 %copy-done = bf16[2,96,640]{2,1,0:T(8,128)(2,1)S(1)} copy-done((bf16[2,96,640]{2,1,0:T(8,128)(2,1)S(1)}, bf16[2,96,640]{2,1,0:T(8,128)(2,1)}, u32[]{:S(2)}) %copy-start) | copy-done | bytes 245784
  1.8 0.0 copy-start.1
  1.8 0.9 %copy-done.1 = bf16[96,640]{1,0:T(8,128)(2,1)S(1)} copy-done((bf16[96,640]{1,0:T(8,128)(2,1)S(1)}, bf16[96,640]{1,0:T(8,128)(2,1)}, u32[]{:S(2)}) %copy-start.1) | copy-done | bytes 122904
  2.7 77.6 %band_block.1 = bf16[96,1280]{1,0:T(8,128)(2,1)S(1)} custom-call(bf16[96,640]{1,0:T(8,128)(2,1)S(1)} %copy-done.1, bf16[2,96,640]{2,1,0:T(8,128)(2,1)S(1)} %copy-done, bf16[48,640]{1,0:T(8,128)(2,1)S(1)} %pad.4.w_ref), custom_call_target="tpu_custom_call" | custom-call | flops 2000000000 | bytes 1000000 | tf_op jit(solution)/shard_map/band_block/pallas_call | solution.py:337
  80.2 0.7 copy.5
Async XLA Ops:
  0.8 0.9 %copy-start = (bf16[2,96,640]{2,1,0:T(8,128)(2,1)S(1)}, bf16[2,96,640]{2,1,0:T(8,128)(2,1)}, u32[]{:S(2)}) copy-start(bf16[2,96,640]{2,1,0:T(8,128)(2,1)} %kv_ref.1) | copy-start | bytes 737284
  1.8 0.9 %copy-start.1 = (bf16[96,640]{1,0:T(8,128)(2,1)S(1)}, bf16[96,640]{1,0:T(8,128)(2,1)}, u32[]{:S(2)}) copy-start(bf16[96,640]{1,0:T(8,128)(2,1)} %q_ref.1) | copy-start | bytes 368644

commit v2 on v1

v2 whole, which is shorter than its diff:
```python
import jax
import jax.numpy as jnp
from jax import lax
from jax.experimental import pallas as pl
from jax.experimental.pallas import tpu as pltpu
from jax.sharding import PartitionSpec as P

HD = 128
TPF = 32
NY = 8
NZ = 8
LOCAL_HEADS = 5
ROWS = 96
UNIT = 768
WINDOW = 2816
SUB = 256
KEYS = 2304
COLS = 40
QUARTER = NY // 2
WROWS = 208
NEG = -1e30
LOGE = 1.4426950408889634
MESH = pl.DeviceIdType.MESH


def on_core(q_ref, kv_ref, w_ref, out_ref,
            kv_win, q_win, o_buf, scores, a_buf, w_own, wbuf, full, part, c_in, summed, x_in, spread,
            w_sem, p1_s, kv_r, q_r, h_s, h_r, w1_s, w1_r, w2_s, w2_r, o_s, o_r, f_s, c_s, c_r, x_s, x_r):
    frames = lax.axis_index("frames")
    heads = lax.axis_index("heads")
    xl = lax.rem(frames, 2)
    y = lax.rem(lax.div(frames, 2), NY)
    z = lax.div(frames, 2 * NY)
    xh = lax.div(heads, 2)
    core = lax.rem(heads, 2)
    par = lax.rem(y, 2)
    fourth = lax.div(y, 2)

    def dev(zz, yy, xx, hh, cc):
        return ((zz * NY + yy) * 2 + xx, hh * 2 + cc)

    def remote(src, dst, send, recv, device):
        return pltpu.make_async_remote_copy(
            src_ref=src, dst_ref=dst, send_sem=send, recv_sem=recv,
            device_id=device, device_id_type=MESH)

    own_copy = pltpu.make_async_copy(w_ref, w_own, w_sem)
    own_copy.start()

    mine = (y * 2 + xl) * 2 + core
    partner = dev(z, y, xl, xh, 1 - core)
    barrier = pltpu.get_barrier_semaphore()

    def greet(device):
        pl.semaphore_signal(barrier, inc=1, device_id=device, device_id_type=MESH)

    for k in range(1, 32):
        other = lax.rem(mine + k, 32)
        greet(dev(z, lax.div(other, 4), lax.rem(lax.div(other, 2), 2), xh, lax.rem(other, 2)))
    for k in range(1, NZ):
        greet(dev(lax.rem(z + k, NZ), y, xl, xh, core))
    for k in (1, NZ - 1):
        greet(dev(lax.rem(z + k, NZ), y, xl, xh, 1 - core))
    for k in range(8):
        greet(dev(z, y - par + k // 4, lax.rem(k // 2, 2), 1 - xh, k % 2))
    spread[...] = jnp.zeros_like(spread)
    for i in range(4):
        for yy in range(QUARTER):
            rows = lax.broadcasted_iota(jnp.int32, (32, 640), 0)
            cols = lax.broadcasted_iota(jnp.int32, (32, 640), 1)
            first = (4 * yy + i) * COLS
            hit = jnp.where(cols == rows + first, 1.0, 0.0).astype(jnp.bfloat16)
            rows, cols = rows[:16], cols[:16]
            tail = jnp.where(cols == lax.rem(rows, 8) + (first + 32), 1.0, 0.0).astype(jnp.bfloat16)
            for zz in (0, 1):
                spread[zz, i, pl.ds(yy * 32, 32), :] = hit
                spread[zz, i, pl.ds(128 + zz * 64 + yy * 16, 16), :] = tail

    own_copy.wait()

    def tails(k, other):
        low = w_own[32:40, k * HD:(k + 1) * HD].astype(jnp.float32)
        high = jnp.zeros_like(low) if other is None else w_own[32:40, other * HD:(other + 1) * HD].astype(jnp.float32)
        return jnp.concatenate([low, high], axis=0).astype(jnp.bfloat16)

    def heads_of(k):
        return w_own[0:32, k * HD:(k + 1) * HD]

    wbuf[z, fourth, 0:32] = heads_of(0)
    wbuf[z, fourth, 32:48] = tails(0, 1)
    wbuf[z, fourth, 48:80] = heads_of(1)
    wbuf[z, fourth, 80:112] = heads_of(2)
    wbuf[z, fourth, 112:128] = tails(2, 3)
    wbuf[z, fourth, 128:160] = heads_of(3)
    wbuf[z, fourth, 160:192] = heads_of(4)
    wbuf[z, fourth, 192:208] = tails(4, None)
    pl.semaphore_wait(barrier, 31 + 7 + 2 + 8)

    slot = lax.rem(y, 4) * 2 + xl
    dest_core = lax.div(y, 4)
    def to_heads(a):
        wanted = core * LOCAL_HEADS + a
        yd, xd = lax.div(lax.div(wanted, 2) * 8, 5), lax.rem(wanted, 2)
        own = (yd == y) & (xd == xl) & (dest_core == core)
        return own, dev(z, yd, xd, xh, dest_core)

    def send_kv(a):
        own, target = to_heads(a)
        src = kv_ref.at[:, :, pl.ds(a * HD, HD)]
        dst = kv_win.at[:, pl.ds(pl.multiple_of(1024 + slot * ROWS, 32), ROWS), :]

        @pl.when(own)
        def _():
            pltpu.make_async_copy(src, dst, kv_r.at[slot]).start()

        @pl.when(jnp.logical_not(own))
        def _():
            remote(src, dst, p1_s.at[a], kv_r.at[slot], target).start()

    def send_q(a):
        own, target = to_heads(a)
        src = q_ref.at[:, pl.ds(a * HD, HD)]
        dst = q_win.at[pl.ds(pl.multiple_of(slot * ROWS, 32), ROWS), :]

        @pl.when(own)
        def _():
            pltpu.make_async_copy(src, dst, q_r.at[slot]).start()

        @pl.when(jnp.logical_not(own))
        def _():
            remote(src, dst, p1_s.at[LOCAL_HEADS + a], q_r.at[slot], target).start()

    def first_step(k):
        ref = wbuf.at[z, fourth]
        return remote(ref, ref, w1_s.at[k - 1], w1_r.at[k - 1],
                      dev(z, lax.rem(y + 2 * k, NY), xl, xh, core))

    def send_w():
        for k in range(1, QUARTER):
            first_step(k).start()

    pair = lax.div(y * 5 + 7, 8)
    head = pair * 2 + xl
    active = (lax.div(pair * 8, 5) == y) & (pair < LOCAL_HEADS)
    unit = z * 2 + core

    def unit_dev(shift):
        other = lax.rem(unit + shift + 16, 16)
        return dev(lax.div(other, 2), y, xl, xh, lax.rem(other, 2))

    halos = tuple((1024 + 192 * r, 192, 256 + 192 * r, 1) for r in range(4))
    halos += tuple((1024 + 192 * r, 192, 1792 + 192 * r, -1) for r in range(4))
    halos += ((1536, 256, 0, 2), (1024, 256, 2560, -2))

    def halo(i):
        start, size, to, shift = halos[i]
        return remote(kv_win.at[:, pl.ds(start, size), :], kv_win.at[:, pl.ds(to, size), :],
                      h_s.at[i], h_r.at[i], unit_dev(shift))

    def send_halos():
        @pl.when(active)
        def _():
            for r in range(4):
                for j in (2 * r, 2 * r + 1):
                    ref = kv_win.at[:, pl.ds(1024 + j * ROWS, ROWS), :]
                    remote(ref, ref, kv_r.at[j], kv_r.at[j], partner).wait_recv()
                halo(r).start()
                halo(4 + r).start()
                if r == 1:
                    halo(9).start()
                elif r == 3:
                    halo(8).start()

    sign = 1 - 2 * core

    def way_of(i):
        return (i, sign) if i < 4 else (i - 4, -sign)

    def ring(i):
        t, way = way_of(i)
        ref = wbuf.at[lax.rem(z - way * t + 2 * NZ, NZ)]
        return remote(ref, ref, w2_s.at[i], w2_r.at[i],
                      dev(lax.rem(z + way + NZ, NZ), y, xl, xh, core))

    def ring_arrival(i):
        t, way = way_of(i)
        ref = wbuf.at[lax.rem(z - way * (t + 1) + 2 * NZ, NZ)]
        remote(ref, ref, w2_r.at[i], w2_r.at[i], partner).wait_recv()

    def start_rings():
        for k in range(1, QUARTER):
            ref = wbuf.at[z, lax.rem(fourth - k + QUARTER, QUARTER)]
            remote(ref, ref, w1_r.at[k - 1], w1_r.at[k - 1], partner).wait_recv()
        ring(0).start()
        ring(4).start()

    def ring_step(t):
        for first, last in ((0, 3), (4, 6)):
            i = first + t
            if i < last:
                ring_arrival(i)
                ring(i + 1).start()
            elif i == last:
                ring_arrival(i)

    def attend(s):
        queries = q_win[pl.ds(s * SUB, SUB), :]
        top = jnp.full((SUB, 256), NEG, jnp.float32)
        rows = lax.broadcasted_iota(jnp.int32, (SUB, 256), 0) // TPF
        cols = lax.broadcasted_iota(jnp.int32, (SUB, 256), 1) // TPF
        for n in range(KEYS // 256):
            keys = kv_win[0, pl.ds(s * SUB + n * 256, 256), :]
            block = lax.dot_general(queries, keys, (((1,), (1,)), ((), ())),
                                    preferred_element_type=jnp.float32)
            if n == 0:
                block = jnp.where(cols >= rows, block, NEG)
            elif n == KEYS // 256 - 1:
                block = jnp.where(cols <= rows, block, NEG)
            scores[:, pl.ds(n * 256, 256)] = block
            top = jnp.maximum(top, block)
        peak = jnp.max(top, axis=1, keepdims=True)
        total = jnp.zeros((SUB, 256), jnp.float32)
        acc = jnp.zeros((SUB, HD), jnp.float32)
        for n in range(KEYS // 256):
            weights = jnp.exp2((scores[:, pl.ds(n * 256, 256)] - peak) * (LOGE * HD ** -0.5))
            total = total + weights
            values = kv_win[1, pl.ds(s * SUB + n * 256, 256), :]
            acc = acc + jnp.dot(weights.astype(jnp.bfloat16), values,
                                preferred_element_type=jnp.float32)
        norm = jnp.sum(total, axis=1, keepdims=True)
        o_buf[pl.ds(s * SUB, SUB), :] = (acc / norm).astype(jnp.bfloat16)

    home_core = lax.div(head, LOCAL_HEADS)
    home_head = lax.rem(head, LOCAL_HEADS)

    def home(r, i):
        yy = core * 4 + r * 2 + i
        own = (yy == y) & (home_core == core)
        src = o_buf.at[pl.ds(r * 384, 384), :]
        dst = a_buf.at[:, pl.ds(pl.multiple_of(home_head * HD, HD), HD)]
        return own, src, dst, dev(z, yy, xl, xh, home_core)

    def send_rows(r):
        for i in (0, 1):
            own, src, dst, target = home(r, i)

            @pl.when(own)
            def _():
                pltpu.make_async_copy(src, dst, o_r.at[home_head]).start()

            @pl.when(jnp.logical_not(own))
            def _():
                remote(src, dst, o_s.at[r * 2 + i], o_r.at[home_head], target).start()

    def from_here(a):
        return lax.rem(core * LOCAL_HEADS + a, 2) == xl

    def hand_on(a):
        ref = a_buf.at[:, pl.ds(a * HD, HD)]
        return remote(ref, ref, f_s.at[a], o_r.at[a], dev(z, y, 1 - xl, xh, core))

    def hand_on_rows():
        for a in range(LOCAL_HEADS):
            @pl.when(from_here(a))
            def _():
                hand_on(a).wait_recv()
                hand_on(a).start()

    def wait_window():
        @pl.when(active)
        def _():
            for j in range(8):
                ref = q_win.at[pl.ds(j * ROWS, ROWS), :]
                remote(ref, ref, q_r.at[j], q_r.at[j], partner).wait_recv()
            for i in range(10):
                halo(i).wait_recv()

    def step(s):
        @pl.when(active)
        def _():
            attend(s)
            for r in ((), (0,), (1,))[s]:
                send_rows(r)

    def kv_sent():
        for a in range(LOCAL_HEADS):
            @pl.when(jnp.logical_not(to_heads(a)[0]))
            def _():
                kv_src = kv_ref.at[:, :, pl.ds(a * HD, HD)]
                remote(kv_src, kv_src, p1_s.at[a], p1_s.at[a], partner).wait_send()

    send_w()
    for a in range(LOCAL_HEADS):
        send_kv(a)
    start_rings()
    send_halos()
    for a in range(LOCAL_HEADS):
        send_q(a)
    ring_step(0)
    wait_window()
    for s in range(3):
        step(s)
    ring_step(1)
    hand_on_rows()
    ring_step(2)

    def wait_rows():
        for a in range(LOCAL_HEADS):
            @pl.when(jnp.logical_not(from_here(a)))
            def _():
                hand_on(a).wait_recv()

    def project(block):
        dims = (((1,), (1,)), ((), ()))

        def piece(start, size):
            return wbuf[pl.ds(block * 2, 2), :, start:start + size].reshape(2 * QUARTER * size, HD)

        main = jnp.concatenate([piece(start, 32) for start in (0, 48, 80, 128, 160)], axis=1)
        ends = [piece(start, 16) for start in (32, 112, 192)]
        a = [a_buf[:, k * HD:(k + 1) * HD] for k in range(LOCAL_HEADS)]
        left = lax.dot_general(a_buf[...], main, dims, preferred_element_type=jnp.float32)
        even = lax.dot_general(jnp.concatenate([a[0], a[2], a[4]], axis=1), jnp.concatenate(ends, axis=1),
                               dims, preferred_element_type=jnp.float32)
        odd = lax.dot_general(jnp.concatenate([a[1], a[3]], axis=1), jnp.concatenate(ends[:2], axis=1),
                              dims, preferred_element_type=jnp.float32)
        lanes = lax.broadcasted_iota(jnp.int32, even.shape, 1)
        return jnp.concatenate([left, jnp.where(lax.rem(lanes, 16) < 8, even, odd)], axis=1)

    half, odd = lax.div(z, 2), lax.rem(z, 2)
    blocks = [half, lax.rem(half + 3 + 2 * odd, 4), lax.rem(half + 1 + 2 * odd, 4), lax.rem(half + 2, 4)]
    out_slot = (par * 2 + xl) * 2 + xh

    def swap(s):
        return remote(part.at[s], c_in.at[s], c_s.at[s], c_r.at[s], partner)

    def scatter(s, kl):
        kh, kc = lax.div(blocks[s], 2), lax.rem(blocks[s], 2)
        here = (kh == xh) & (kc == core) & (core == par) & (kl == xl)
        src = summed.at[s, pl.ds(kl * ROWS, ROWS), :]
        return here, remote(src, x_in.at[out_slot], x_s.at[s * 2 + kl], x_r.at[out_slot],
                            dev(z, y - par + core, kl, kh, kc))

    def begin(s):
        full[s] = project(blocks[s])
        part[s] = full[s, pl.ds(pl.multiple_of((1 - core) * 192, 64), 192), :].astype(jnp.bfloat16)
        swap(s).start()

    def finish(s):
        swap(s).wait_recv()
        own = full[s, pl.ds(pl.multiple_of(core * 192, 64), 192), :]
        summed[s] = (own + c_in[s].astype(jnp.float32)).astype(jnp.bfloat16)
        for kl in (0, 1):
            here, copy = scatter(s, kl)

            @pl.when(here)
            def _():
                x_in[out_slot] = summed[s, pl.ds(kl * ROWS, ROWS), :]

            @pl.when(jnp.logical_not(here))
            def _():
                copy.start()

    wait_rows()
    begin(0)
    begin(1)
    finish(0)
    begin(2)
    finish(1)
    ring_step(3)
    begin(3)
    finish(2)
    finish(3)

    for i in range(8):
        @pl.when((i != out_slot) | (core != par))
        def _():
            remote(x_in.at[i], x_in.at[i], x_r.at[i], x_r.at[i], partner).wait_recv()
    for zz in (0, 1):
        total = None
        for i in range(4):
            rows = x_in[2 * i:2 * i + 2].reshape(2 * ROWS, 384)
            rows = jnp.concatenate([rows[:, zz * 128:(zz + 1) * 128], rows[:, 256:]], axis=1)
            piece = jnp.dot(rows, spread[zz, i], preferred_element_type=jnp.float32)
            total = piece if total is None else total + piece
        out_ref[:, pl.ds(zz * 640, 640)] = (total[:ROWS] + total[ROWS:]).astype(jnp.bfloat16)

    for a in range(LOCAL_HEADS):
        @pl.when(jnp.logical_not(to_heads(a)[0]))
        def _():
            q_src = q_ref.at[:, pl.ds(a * HD, HD)]
            remote(q_src, q_src, p1_s.at[LOCAL_HEADS + a], p1_s.at[LOCAL_HEADS + a], partner).wait_send()
    kv_sent()
    for k in range(1, QUARTER):
        first_step(k).wait_send()
    for i in range(7):
        ring(i).wait_send()

    @pl.when(active)
    def _():
        for i in range(10):
            halo(i).wait_send()
        for r in (0, 1):
            for k in (0, 1):
                own, src, dst, target = home(r, k)

                @pl.when(jnp.logical_not(own))
                def _():
                    remote(src, dst, o_s.at[r * 2 + k], o_s.at[r * 2 + k], target).wait_send()
    for a in range(LOCAL_HEADS):
        @pl.when(from_here(a))
        def _():
            hand_on(a).wait_send()
    for s in range(4):
        swap(s).wait_send()
        for kl in (0, 1):
            here, copy = scatter(s, kl)

            @pl.when(jnp.logical_not(here))
            def _():
                copy.wait_send()


def on_device(queries, keys_values, out_weight):
    bf16 = jnp.bfloat16
    vmem = pl.BlockSpec(memory_space=pltpu.VMEM)
    dma = pltpu.SemaphoreType.DMA
    return pl.pallas_call(
        on_core,
        out_shape=jax.ShapeDtypeStruct((ROWS, 1280), bf16),
        in_specs=[pl.BlockSpec(memory_space=pl.ANY)] * 3,
        out_specs=vmem,
        scratch_shapes=[
            pltpu.VMEM((2, WINDOW, HD), bf16),
            pltpu.VMEM((UNIT, HD), bf16),
            pltpu.VMEM((UNIT, HD), bf16),
            pltpu.VMEM((SUB, KEYS), jnp.float32),
            pltpu.VMEM((384, 640), bf16),
            pltpu.VMEM((COLS, 640), bf16),
            pltpu.VMEM((NZ, QUARTER, WROWS, HD), bf16),
            pltpu.VMEM((4, 384, 384), jnp.float32),
            pltpu.VMEM((4, 192, 384), bf16),
            pltpu.VMEM((4, 192, 384), bf16),
            pltpu.VMEM((4, 192, 384), bf16),
            pltpu.VMEM((8, ROWS, 384), bf16),
            pltpu.VMEM((2, 4, 256, 640), bf16),
            dma, dma((10,)), dma((8,)), dma((8,)), dma((10,)), dma((10,)),
            dma((3,)), dma((3,)), dma((7,)), dma((7,)),
            dma((4,)), dma((5,)), dma((5,)), dma((4,)), dma((4,)), dma((8,)), dma((8,)),
        ],
        compiler_params=pltpu.CompilerParams(
            collective_id=0, has_side_effects=True, vmem_limit_bytes=62 * 2 ** 20),
        cost_estimate=pl.CostEstimate(flops=2 * 10 ** 9, bytes_accessed=10 ** 6, transcendentals=2 * 10 ** 6),
        name="band_block",
    )(queries, keys_values, out_weight.T)


def solution(mesh):
    in_specs = (P("frames", "heads"), P(None, "frames", "heads"), P("heads", "frames"))
    out_specs = P("frames", "heads")
    return jax.shard_map(
        on_device, mesh=mesh, in_specs=in_specs, out_specs=out_specs, check_vma=False
    )
```

time: 81.4 us -> 69.3 us (0.85)
  the two profiles are of different devices: /device:TPU:1 before, /device:TPU:54 now
where the time goes in v2:
time: 69.3 us; the launch traced here: 69.1 us
  Pallas kernels  67.4 us (97%)
  local copies, waits for them, and re-layouts  1.65 us (2%)
    pallas_call x1, Pallas kernels, on_device(): pl.pallas_call(on_core, out_shape=jax.ShapeDtypeStruct((ROWS, 1280), bf16...  67.4 us
    unnamed x1, local copies, waits for them, and re-layouts  1.65 us

profile of v2, /device:TPU:54, one launch (start us, length us, event | category | flops | bytes accessed | tf_op | source)
XLA Modules:
  0.0 69.1 jit_solution(2162689142684115903)
XLA Ops:
  0.0 67.4 %band_block.1 = bf16[96,1280]{1,0:T(8,128)(2,1)} custom-call(bf16[96,640]{1,0:T(8,128)(2,1)} %q_ref.1, bf16[2,96,640]{2,1,0:T(8,128)(2,1)} %kv_ref.1, bf16[40,640]{1,0:T(8,128)(2,1)} %bitcast.1), custom_call_target="tpu_custom_call" | custom-call | flops 2000000000 | bytes 1000000 | tf_op jit(solution)/shard_map/band_block/pallas_call | solution.py:428
  67.4 1.7 %copy.5 = bf16[96,1280]{1,0:T(8,128)(2,1)} copy(bf16[96,1280]{1,0:T(8,128)(2,1)} %band_block.1) | data formatting | bytes 491520

commit v3 on v2

--- a/solution.py
+++ b/solution.py
@@ -296,8 +296,8 @@
     send_halos()
     for a in range(LOCAL_HEADS):
         send_q(a)
+    wait_window()
     ring_step(0)
-    wait_window()
     for s in range(3):
         step(s)
     ring_step(1)

time: 69.3 us -> 67.4 us (0.973)
  the two profiles are of different devices: /device:TPU:54 before, /device:TPU:1 now
where the time goes in v3:
time: 67.4 us; the launch traced here: 67.2 us
  Pallas kernels  65.5 us (97%)
  local copies, waits for them, and re-layouts  1.65 us (2%)
    pallas_call x1, Pallas kernels, on_device(): pl.pallas_call(on_core, out_shape=jax.ShapeDtypeStruct((ROWS, 1280), bf16...  65.5 us
    unnamed x1, local copies, waits for them, and re-layouts  1.65 us

profile of v3, /device:TPU:1, one launch (start us, length us, event | category | flops | bytes accessed | tf_op | source)
XLA Modules:
  0.0 67.2 jit_solution(17719003550147682486)
XLA Ops:
  0.0 65.5 %band_block.1 = bf16[96,1280]{1,0:T(8,128)(2,1)} custom-call(bf16[96,640]{1,0:T(8,128)(2,1)} %q_ref.1, bf16[2,96,640]{2,1,0:T(8,128)(2,1)} %kv_ref.1, bf16[40,640]{1,0:T(8,128)(2,1)} %bitcast.1), custom_call_target="tpu_custom_call" | custom-call | flops 2000000000 | bytes 1000000 | tf_op jit(solution)/shard_map/band_block/pallas_call | solution.py:428
  65.5 1.7 %copy.5 = bf16[96,1280]{1,0:T(8,128)(2,1)} copy(bf16[96,1280]{1,0:T(8,128)(2,1)} %band_block.1) | data formatting | bytes 491520
